TPU v7x, 256 devices: a whole 4x4x8 slice. The times are simulated.
256 devices in a mesh: patch: 16 (over z_lo, x), head: 16 (over z_hi, y, core).
Axes of the slice: x: 4, y: 4, z: 8 (z_hi: 2, z_lo: 4; z = z_hi * 4 + z_lo), core: 2. Of those that a mesh axis runs over, the one named last changes fastest.
Arguments:
- queries: bfloat16 [2048, 6144], P('patch', 'head'), may hold values from -17 to 17
- stale_kv: float32 [2, 2048, 6144], P(None, None, 'head'), may hold values from -8 to 8, as said below
- delta_kv: bfloat16 [2, 2048, 6144], P(None, 'patch', 'head'), may hold values from -17 to 17
- out_weight: bfloat16 [6144, 6144], P('head'), may hold values from -0.078125 to 0.078125
Outputs:
- projected: bfloat16 [2048, 6144], P(('patch', 'head'))
Inputs may be any that keep to these rules, and one draw needn't show every extreme that they name: `stale_kv`: stored keys and values of order one.
All inputs are finite; a program needn't handle non-finite values.
Results may differ from a plain program's by a relative error of at most 0.019.
Values may be sent and summed in bfloat16 or wider, within the bound.
A program may use at most 64 MiB of HBM per device.

v0:
```python
import math

import jax
import jax.numpy as jnp
from jax import lax
from jax.sharding import PartitionSpec as P

HD = 128


def split_heads(tensor, head_count):
    return tensor.reshape(tensor.shape[0], head_count, HD)


def block_scores(query_split, key_value, head_count):
    keys_split = split_heads(key_value[0], head_count)
    values_split = split_heads(key_value[1], head_count)
    scores = jnp.einsum(
        "qhd,khd->hqk", query_split, keys_split, preferred_element_type=jnp.float32
    ) * (1.0 / math.sqrt(HD))
    return (scores, values_split)


def weighted(expo, values_split):
    return jnp.einsum(
        "hqk,khd->hqd", expo.astype(jnp.bfloat16), values_split, preferred_element_type=jnp.float32
    )


def finish(accum, denom):
    ratio = accum / denom[:, :, None]
    return (
        jnp.transpose(ratio, (1, 0, 2))
        .reshape(ratio.shape[1], ratio.shape[0] * HD)
        .astype(jnp.bfloat16)
    )


def body(queries, stale_kv, delta_kv, out_weight):
    tok_rows, col_width = queries.shape
    head_count = col_width // HD
    query_split = split_heads(queries, head_count)
    deltas = lax.all_gather(delta_kv, "patch", axis=1, tiled=True)
    refreshed = (stale_kv + deltas.astype(jnp.float32)).astype(jnp.bfloat16)
    scores, values_split = block_scores(query_split, refreshed, head_count)
    peak = jnp.max(scores, axis=2, keepdims=True)
    expo = jnp.exp(scores - peak)
    attended = finish(weighted(expo, values_split), jnp.sum(expo, axis=2))
    return lax.psum_scatter(
        jnp.dot(attended, out_weight, preferred_element_type=jnp.float32).astype(jnp.bfloat16),
        "head",
        scatter_dimension=0,
        tiled=True,
    )


def solution(mesh):
    return jax.shard_map(
        body,
        mesh=mesh,
        in_specs=(
            P("patch", "head"),
            P(None, None, "head"),
            P(None, "patch", "head"),
            P("head", None),
        ),
        out_specs=P(("patch", "head"), None),
        check_vma=False,
    )
```

profile of v0, /device:TPU:1, one launch (start us, length us, event | category | flops | bytes accessed | tf_op | source)
XLA Modules:
  0.0 193.1 jit_solution(12342612237156547760)
XLA Ops:
  6.5 0.0 all-gather.2.cloned.1.call-start
  6.5 1.7 copy.8
  8.3 0.0 all-gather.2.cloned.1.call-update
  8.3 0.0 copy-start
  8.3 0.0 reduce-scatter.2.cloned.1.call-start
  8.4 6.6 %copy.9 = f32[2,2048,384]{1,2,0:T(8,128)} copy(f32[2,2048,384]{2,1,0:T(8,128)} %param.5) | data formatting | bytes 12582912 | tf_op args[1]
  15.0 0.0 copy-done
  15.0 0.1 copy.10
  15.1 70.7 %all-gather.2.cloned.1.call-done = bf16[2,2048,384]{1,2,0:T(8,128)(2,1)} async-done(((bf16[2,128,384]{1,2,0:T(8,128)(2,1)}), bf16[2,2048,384]{1,2,0:T(8,128)(2,1)}) %all-gather.2.cloned.1.call-update) | async-done | bytes 3145744 | tf_op jit(solution)/shard_map/all_gather | solution.py:43
  85.8 4.8 %add_convert_fusion = bf16[2,2048,384]{1,2,0:T(8,128)(2,1)S(1)} fusion(f32[2,2048,384]{1,2,0:T(8,128)} %copy.9, bf16[2,2048,384]{1,2,0:T(8,128)(2,1)} %all-gather.2.cloned.1.call-done), kind=kLoop, calls=%fused_computation.1 | loop fusion | flops 4718592 | bytes 12582912 | tf_op jit(solution)/shard_map/convert_element_type | solution.py:44
  90.6 0.2 fusion.15
  90.8 0.0 slice-start
  90.9 0.7 bitcast_reduce_fusion
  91.6 0.0 slice-start.1
  91.6 0.4 fusion.1
  92.0 0.7 fusion.12
  92.8 0.3 slice-done
  93.0 0.3 slice-done.1
  93.3 2.2 %convolution_convert_fusion = bf16[128,6144]{1,0:T(8,128)(2,1)} fusion(bf16[128,384]{0,1:T(8,128)(2,1)S(1)} %bitcast.36, bf16[384,6144]{1,0:T(8,128)(2,1)S(1)} %bitcast.33), kind=kOutput, calls=%fused_computation | convolution fusion | flops 604766208 | bytes 6389760 | tf_op jit(solution)/shard_map/dot_general | solution.py:50
  95.5 0.0 reduce-scatter.2.cloned.1.call-update
  95.6 90.7 %reduce-scatter.2.cloned.1.call-done = bf16[8,6144]{1,0:T(8,128)(2,1)} async-done(((bf16[128,6144]{1,0:T(8,128)(2,1)}), bf16[8,6144]{1,0:T(8,128)(2,1)}) %reduce-scatter.2.cloned.1.call-update) | async-done | bytes 98320 | tf_op jit(solution)/shard_map/reduce_scatter | solution.py:49
  (1 shorter events, 0.0 us)
Async XLA Ops:
  6.5 79.3 %all-gather.2.cloned.1.call-start = ((), (), s32[]{:S(2)}) async-start(), calls=%async_computation.1 | async-start | bytes 3342336 | tf_op jit(solution)/shard_map/all_gather | solution.py:43
  8.3 6.7 %copy-start = (bf16[128,384]{1,0:T(8,128)(2,1)S(1)}, bf16[128,384]{1,0:T(8,128)(2,1)}, u32[]{:S(2)}) copy-start(bf16[128,384]{1,0:T(8,128)(2,1)} %param.4) | copy-start | bytes 294916
  8.3 178.0 %reduce-scatter.2.cloned.1.call-start = ((), (), s32[]{:S(2)}) async-start(), calls=%async_computation.2 | async-start | bytes 1671168 | tf_op jit(solution)/shard_map/reduce_scatter | solution.py:49
  90.8 2.2 %slice-start = ((s8[4718592]{0:T(1024)(128)(4,1)}), s8[4194304]{0:T(1024)(128)(4,1)S(1)}, s32[]{:S(2)}) async-start(s8[4718592]{0:T(1024)(128)(4,1)} %bitcast.32), calls=%async_computation.3 | async-start | bytes 8388608
  91.6 1.8 slice-start.1
Sparse Core Ops, SparseCore 0:
  9.1 76.6 all-gather.1
  95.7 90.5 reduce-scatter.1
where the time goes:
time: 194 us; the launch traced here: 193 us
  waiting for transfers between devices  161 us (83%)
  between operations  13.5 us (7%)
  local copies, waits for them, and re-layouts  9.31 us (5%)
  other arithmetic  5.24 us (3%)
  matrix products  3.65 us (2%)
    reduce_scatter x1, waiting for transfers between devices, body(): lax.psum_scatter(jnp.dot(attended, out_weight, preferred_element_type=jnp...  90.7 us
    all_gather x1, waiting for transfers between devices, body(): deltas = lax.all_gather(delta_kv, 'patch', axis=1, tiled=True)  70.7 us
    unnamed x9, local copies, waits for them, and re-layouts  9.09 us
    convert_element_type x1, other arithmetic, body(): refreshed = (stale_kv + deltas.astype(jnp.float32)).astype(jnp.bfloat16)  4.8 us
  transfers between devices with their start and end apart: 2, of which 2 were waited for; matrix products, arithmetic and copies ran while one was open for 4% of the time, Pallas kernels for 0%

commit v1 on v0

v1 whole, which is shorter than its diff:
```python
import functools
import math

import jax
import jax.numpy as jnp
from jax import lax
from jax.experimental import pallas as pl
from jax.experimental.pallas import tpu as pltpu
from jax.sharding import PartitionSpec as P

MESH = pl.DeviceIdType.MESH
F32, BF16 = jnp.float32, jnp.bfloat16

HD = 128
HEADS = 3
TOK = 128
RING = 4
COLS = HEADS * HD
D = 6144
CHUNKS = 6
WIDTH = D // CHUNKS
PART = HD + 16
SCALE = 1.0 / math.sqrt(HD)


def split3(value):
    high = value.astype(BF16).astype(F32)
    rest = value - high
    middle = rest.astype(BF16).astype(F32)
    return high, middle, rest - middle


def kernel(
    q_ref, stale_ref, delta_ref, w_ref, out_ref,
    stale_v, kv, qs, part_out, part_in, w_v, att, own, sib_out, sib_in, y_out, y_in, z_own, z_out, z_in,
    local_sem, kv_s, kv_r, q_s, q_r, o_s, o_r, sib_s, sib_r, y_s, y_r, z_s, z_r,
):
    patch, head = lax.axis_index("patch"), lax.axis_index("head")
    z, x = patch // RING, lax.rem(patch, RING)
    z_hi, y, core = head // 8, lax.rem(head // 2, RING), lax.rem(head, 2)

    def at_x(k):
        return (z * RING + lax.rem(x + k + RING, RING), head)

    def at_z(k):
        return (lax.rem(z + k + RING, RING) * RING + x, head)

    def at_y(k):
        return (patch, z_hi * 8 + lax.rem(y + k, RING) * 2 + core)

    sibling = (patch, z_hi * 8 + y * 2 + (1 - core))
    across = (patch, (1 - z_hi) * 8 + y * 2 + core)

    def remote(src, dst, send, recv, device):
        return pltpu.make_async_remote_copy(
            src_ref=src, dst_ref=dst, send_sem=send, recv_sem=recv, device_id=device, device_id_type=MESH
        )

    local = []
    for k in range(RING):
        row = (z * RING + lax.rem(x - k + RING, RING)) * TOK
        local.append(pltpu.make_async_copy(stale_ref.at[:, pl.ds(row, TOK), :], stale_v.at[k], local_sem.at[k]))
    for h in range(HEADS):
        cols = pl.ds(h * HD, HD)
        local.append(pltpu.make_async_copy(delta_ref.at[:, :, cols], kv.at[h, 0], local_sem.at[4 + h]))
        local.append(pltpu.make_async_copy(q_ref.at[:, cols], qs.at[h, 0], local_sem.at[7 + h]))
    weight = pltpu.make_async_copy(w_ref, w_v, local_sem.at[10])
    for copy in local:
        copy.start()
    weight.start()

    barrier = pltpu.get_barrier_semaphore()
    partners = [at_x(k) for k in (1, 2, 3)] + [at_z(k) for k in (1, 2, 3)] + [at_y(k) for k in (1, 2, 3)] + [sibling, across]
    for device in partners:
        pl.semaphore_signal(barrier, inc=1, device_id=device, device_id_type=MESH)
    pl.semaphore_wait(barrier, len(partners))

    kv_copies, q_copies = {}, {}
    for h in range(HEADS):
        cols = pl.ds(h * HD, HD)
        for k in (1, 2, 3):
            kv_copies[h, k] = remote(
                delta_ref.at[:, :, cols], kv.at[h, k], kv_s.at[h, k - 1], kv_r.at[h, k - 1], at_x(k)
            )
            q_copies[h, k] = remote(q_ref.at[:, cols], qs.at[h, k], q_s.at[h, k - 1], q_r.at[h, k - 1], at_z(k))
        for k in (1, 2, 3):
            kv_copies[h, k].start()
            q_copies[h, k].start()

    for copy in local:
        copy.wait()

    o_copies = {}
    for h in range(HEADS):
        cols = slice(h * HD, (h + 1) * HD)
        keys, values = [], []
        for k in range(RING):
            if k:
                kv_copies[h, k].wait_recv()
            fresh = stale_v[k, :, :, cols] + kv[h, k].astype(F32)
            keys.append(fresh[0].astype(BF16))
            values.append(fresh[1].T.astype(BF16))
        keys = jnp.concatenate(keys, axis=0)
        values = jnp.concatenate(values, axis=1)
        for k in (1, 2, 3, 0):
            if k:
                q_copies[h, k].wait_recv()
            scores = lax.dot_general(keys, qs[h, k], (((1,), (1,)), ((), ())), preferred_element_type=F32)
            peak = jnp.max(scores, axis=0, keepdims=True)
            expo = jnp.exp((scores - peak) * SCALE)
            denom = jnp.sum(expo, axis=0, keepdims=True)
            mixed = jnp.dot(values, expo.astype(BF16), preferred_element_type=F32) / denom
            row = lax.broadcasted_iota(jnp.int32, (16, TOK), 0)
            stats = jnp.zeros((16, TOK), F32)
            for i, term in enumerate(split3(peak * SCALE) + split3(denom)):
                stats = jnp.where(row == i, term, stats)
            buffer = part_out if k else part_in
            buffer[h, k, :HD, :] = mixed.astype(BF16)
            buffer[h, k, HD:, :] = stats.astype(BF16)
            if k:
                o_copies[h, k] = remote(
                    part_out.at[h, k], part_in.at[h, k], o_s.at[h, k - 1], o_r.at[h, k - 1], at_z(RING - k)
                )
                o_copies[h, k].start()

    for h in range(HEADS):
        peaks, denoms = [], []
        for k in range(RING):
            if k:
                o_copies[h, k].wait_recv()
            stats = part_in[h, k, HD:, :].astype(F32)
            peaks.append(stats[0:1] + stats[1:2] + stats[2:3])
            denoms.append(stats[3:4] + stats[4:5] + stats[5:6])
        top = functools.reduce(jnp.maximum, peaks)
        shares = [d * jnp.exp(p - top) for p, d in zip(peaks, denoms)]
        total = functools.reduce(jnp.add, shares)
        merged = functools.reduce(
            jnp.add, [part_in[h, k, :HD, :].astype(F32) * (shares[k] / total) for k in range(RING)]
        ).T
        by_core = [
            jnp.concatenate(
                [merged[(zz * 8 + yy * 2 + c) * 8 :][:8] for yy in range(RING) for zz in range(2)], axis=0
            )
            for c in range(2)
        ]
        mine = jnp.where(core == 0, by_core[0], by_core[1])
        other = jnp.where(core == 0, by_core[1], by_core[0])
        att[0:64, h * HD : (h + 1) * HD] = mine.astype(BF16)
        att[64:128, h * HD : (h + 1) * HD] = other.astype(BF16)

    weight.wait()
    sib_copies, y_copies, z_copies = {}, {}, {}

    def project(j):
        cols = slice(j * WIDTH, (j + 1) * WIDTH)
        prod = jnp.dot(att[...], w_v[:, cols], preferred_element_type=F32)
        own[:, :, cols] = prod[:64].reshape(RING, 16, WIDTH)
        sib_out[j] = prod[64:].astype(BF16)
        sib_copies[j] = remote(sib_out.at[j], sib_in.at[j], sib_s.at[j], sib_r.at[j], sibling)
        sib_copies[j].start()

    def to_y(j):
        cols = slice(j * WIDTH, (j + 1) * WIDTH)
        sib_copies[j].wait_recv()
        pair = own[:, :, cols] + sib_in[j].astype(F32).reshape(RING, 16, WIDTH)
        own[:, :, cols] = pair
        y_out[j] = pair.astype(BF16)
        for k in (1, 2, 3):
            y_copies[j, k] = remote(
                y_out.at[j, lax.rem(y + k, RING)], y_in.at[j, k - 1], y_s.at[j, k - 1], y_r.at[j, k - 1], at_y(k)
            )
            y_copies[j, k].start()

    def to_z(j):
        cols = slice(j * WIDTH, (j + 1) * WIDTH)
        total = own[y, :, cols]
        for k in (1, 2, 3):
            y_copies[j, k].wait_recv()
            total = total + y_in[j, k - 1].astype(F32)
        z_own[0, :, cols] = total[:8]
        z_own[1, :, cols] = total[8:]
        half = WIDTH // 2
        away = z_own[1 - z_hi, :, cols]
        z_out[j] = jnp.concatenate([away[:, :half], away[:, half:]], axis=0).astype(BF16)
        z_copies[j] = remote(z_out.at[j], z_in.at[j], z_s.at[j], z_r.at[j], across)
        z_copies[j].start()

    def finish(j):
        z_copies[j].wait_recv()
        half = WIDTH // 2
        for i in range(2):
            cols = slice(j * WIDTH + i * half, j * WIDTH + (i + 1) * half)
            came = z_in[j].astype(F32)[i * 8 : (i + 1) * 8]
            out_ref[:, cols] = (z_own[z_hi, :, cols] + came).astype(BF16)

    stages = (project, to_y, to_z, finish)
    lags = (0, 2, 6, 8)
    for t in range(CHUNKS + lags[-1]):
        for stage, lag in zip(stages, lags):
            if 0 <= t - lag < CHUNKS:
                stage(t - lag)

    for copies in (kv_copies, q_copies, o_copies, sib_copies, y_copies, z_copies):
        for copy in copies.values():
            copy.wait_send()


def body(queries, stale_kv, delta_kv, out_weight):
    dma = pltpu.SemaphoreType.DMA
    return pl.pallas_call(
        kernel,
        name="sublayer",
        out_shape=jax.ShapeDtypeStruct((8, D), BF16),
        in_specs=[pl.BlockSpec(memory_space=pl.ANY)] * 4,
        out_specs=pl.BlockSpec(memory_space=pltpu.VMEM),
        scratch_shapes=[
            pltpu.VMEM((RING, 2, TOK, COLS), F32),
            pltpu.VMEM((HEADS, RING, 2, TOK, HD), BF16),
            pltpu.VMEM((HEADS, RING, TOK, HD), BF16),
            pltpu.VMEM((HEADS, RING, PART, TOK), BF16),
            pltpu.VMEM((HEADS, RING, PART, TOK), BF16),
            pltpu.VMEM((COLS, D), BF16),
            pltpu.VMEM((TOK, COLS), BF16),
            pltpu.VMEM((RING, 16, D), F32),
            pltpu.VMEM((CHUNKS, 64, WIDTH), BF16),
            pltpu.VMEM((CHUNKS, 64, WIDTH), BF16),
            pltpu.VMEM((CHUNKS, RING, 16, WIDTH), BF16),
            pltpu.VMEM((CHUNKS, RING - 1, 16, WIDTH), BF16),
            pltpu.VMEM((2, 8, D), F32),
            pltpu.VMEM((CHUNKS, 16, WIDTH // 2), BF16),
            pltpu.VMEM((CHUNKS, 16, WIDTH // 2), BF16),
            dma((11,)),
            dma((HEADS, 3)),
            dma((HEADS, 3)),
            dma((HEADS, 3)),
            dma((HEADS, 3)),
            dma((HEADS, 3)),
            dma((HEADS, 3)),
            dma((CHUNKS,)),
            dma((CHUNKS,)),
            dma((CHUNKS, 3)),
            dma((CHUNKS, 3)),
            dma((CHUNKS,)),
            dma((CHUNKS,)),
        ],
        compiler_params=pltpu.CompilerParams(
            collective_id=0, has_side_effects=True, vmem_limit_bytes=60 * 1024 * 1024
        ),
    )(queries, stale_kv, delta_kv, out_weight)


def solution(mesh):
    return jax.shard_map(
        body,
        mesh=mesh,
        in_specs=(
            P("patch", "head"),
            P(None, None, "head"),
            P(None, "patch", "head"),
            P("head", None),
        ),
        out_specs=P(("patch", "head"), None),
        check_vma=False,
    )
```

time: 194 us -> 51 us (0.26)
  waiting for transfers between devices: 161 us -> 0 us
  Pallas kernels: 0 us -> 48.4 us
  between operations: 13.5 us -> 0.01 us
  local copies, waits for them, and re-layouts: 9.31 us -> 1.54 us
  other arithmetic: 5.24 us -> 0 us
  matrix products: 3.65 us -> 0 us
    reduce_scatter x1 -> x0, waiting for transfers between devices: 90.7 us -> none  [body(): lax.psum_scatter(jnp.dot(attended, out_weight, preferred_element_type=jnp...]
    all_gather x1 -> x0, waiting for transfers between devices: 70.7 us -> none  [body(): deltas = lax.all_gather(delta_kv, 'patch', axis=1, tiled=True)]
    pallas_call x0 -> x1, Pallas kernels: none -> 48.4 us  [body(): pl.pallas_call(kernel, name='sublayer', out_shape=jax.ShapeDtypeStruct((8...]
    unnamed x9 -> x1, local copies, waits for them, and re-layouts: 9.09 us -> 1.54 us
    convert_element_type x1 -> x0, other arithmetic: 4.8 us -> none  [body(): refreshed = (stale_kv + deltas.astype(jnp.float32)).astype(jnp.bfloat16)]
    dot_general x3 -> x0, matrix products: 3.65 us -> none  [the longest x1 2.21 us: body(): jnp.dot(attended, out_weight, preferred_element_type=jnp.float32)]
  transfers between devices with their start and end apart: 2 -> 0, of which waited for: 2 -> 0; matrix products, arithmetic and copies ran while one was open for 4% -> 0% of each run, Pallas kernels for 0% -> 0%
where the time goes in v1:
time: 51 us; the launch traced here: 50 us
  Pallas kernels  48.4 us (95%)
  local copies, waits for them, and re-layouts  1.54 us (3%)
    pallas_call x1, Pallas kernels, body(): pl.pallas_call(kernel, name='sublayer', out_shape=jax.ShapeDtypeStruct((8...  48.4 us
    unnamed x1, local copies, waits for them, and re-layouts  1.54 us

profile of v1, /device:TPU:1, one launch (start us, length us, event | category | flops | bytes accessed | tf_op | source)
XLA Modules:
  0.0 50.0 jit_solution(13672649327749887630)
XLA Ops:
  0.0 48.4 %sublayer.1 = bf16[8,6144]{1,0:T(8,128)(2,1)} custom-call(bf16[128,384]{1,0:T(8,128)(2,1)} %q_ref.1, f32[2,2048,384]{2,1,0:T(8,128)} %stale_ref.1, bf16[2,128,384]{2,1,0:T(8,128)(2,1)} %delta_ref.1, bf16[384,6144]{1,0:T(8,128)(2,1)} %w_ref.1), custom_call_target="tpu_custom_call" | custom-call | tf_op jit(solution)/shard_map/sublayer/pallas_call | solution.py:210
  48.4 1.5 %copy.6 = bf16[8,6144]{1,0:T(8,128)(2,1)} copy(bf16[8,6144]{1,0:T(8,128)(2,1)} %sublayer.1) | data formatting | bytes 196608

commit v2 on v1

--- a/solution.py
+++ b/solution.py
@@ -17,8 +17,9 @@
 RING = 4
 COLS = HEADS * HD
 D = 6144
-CHUNKS = 6
+CHUNKS = 4
 WIDTH = D // CHUNKS
+HALF = WIDTH // 2
 PART = HD + 16
 SCALE = 1.0 / math.sqrt(HD)
 
@@ -32,7 +33,7 @@
 
 def kernel(
     q_ref, stale_ref, delta_ref, w_ref, out_ref,
-    stale_v, kv, qs, part_out, part_in, w_v, att, own, sib_out, sib_in, y_out, y_in, z_own, z_out, z_in,
+    stale_v, kv, qs, part_out, part_in, w_v, att, own, sib_out, sib_in, y_out, y_in, y_sum, z_own, z_out, z_in,
     local_sem, kv_s, kv_r, q_s, q_r, o_s, o_r, sib_s, sib_r, y_s, y_r, z_s, z_r,
 ):
     patch, head = lax.axis_index("patch"), lax.axis_index("head")
@@ -42,12 +43,13 @@
     def at_x(k):
         return (z * RING + lax.rem(x + k + RING, RING), head)
 
-    def at_z(k):
-        return (lax.rem(z + k + RING, RING) * RING + x, head)
+    def at_z(place):
+        return (place * RING + x, head)
 
     def at_y(k):
-        return (patch, z_hi * 8 + lax.rem(y + k, RING) * 2 + core)
-
+        return (patch, z_hi * 8 + lax.rem(y + k + RING, RING) * 2 + core)
+
+    others = {1: z + 1 - 2 * lax.rem(z, 2), 2: lax.rem(z + 2, RING), 3: 3 - z}
     sibling = (patch, z_hi * 8 + y * 2 + (1 - core))
     across = (patch, (1 - z_hi) * 8 + y * 2 + core)
 
@@ -70,7 +72,7 @@
     weight.start()
 
     barrier = pltpu.get_barrier_semaphore()
-    partners = [at_x(k) for k in (1, 2, 3)] + [at_z(k) for k in (1, 2, 3)] + [at_y(k) for k in (1, 2, 3)] + [sibling, across]
+    partners = [at_x(1), at_x(-1), at_y(1), at_y(-1)] + [at_z(others[k]) for k in (1, 2, 3)] + [sibling, across]
     for device in partners:
         pl.semaphore_signal(barrier, inc=1, device_id=device, device_id_type=MESH)
     pl.semaphore_wait(barrier, len(partners))
@@ -78,14 +80,25 @@
     kv_copies, q_copies = {}, {}
     for h in range(HEADS):
         cols = pl.ds(h * HD, HD)
-        for k in (1, 2, 3):
-            kv_copies[h, k] = remote(
-                delta_ref.at[:, :, cols], kv.at[h, k], kv_s.at[h, k - 1], kv_r.at[h, k - 1], at_x(k)
-            )
-            q_copies[h, k] = remote(q_ref.at[:, cols], qs.at[h, k], q_s.at[h, k - 1], q_r.at[h, k - 1], at_z(k))
-        for k in (1, 2, 3):
-            kv_copies[h, k].start()
-            q_copies[h, k].start()
+        mine, query = delta_ref.at[:, :, cols], q_ref.at[:, cols]
+        kv_copies[h, 1] = remote(mine, kv.at[h, 1], kv_s.at[h, 0], kv_r.at[h, 0], at_x(1))
+        kv_copies[h, 3] = remote(mine, kv.at[h, 3], kv_s.at[h, 1], kv_r.at[h, 1], at_x(-1))
+        for k in (2, 1):
+            q_copies[h, k] = remote(query, qs.at[h, k], q_s.at[h, k - 1], q_r.at[h, k - 1], at_z(others[k]))
+        q_copies[h, 2].start()
+        kv_copies[h, 1].start()
+        kv_copies[h, 3].start()
+        q_copies[h, 1].start()
+    for h in range(HEADS):
+        kv_copies[h, 1].wait_recv()
+        kv_copies[h, "k"] = remote(kv.at[h, 1, 0], kv.at[h, 2, 0], kv_s.at[h, 2], kv_r.at[h, 2], at_x(1))
+        kv_copies[h, "k"].start()
+        kv_copies[h, 3].wait_recv()
+        kv_copies[h, "v"] = remote(kv.at[h, 3, 1], kv.at[h, 2, 1], kv_s.at[h, 3], kv_r.at[h, 3], at_x(-1))
+        kv_copies[h, "v"].start()
+        q_copies[h, 2].wait_recv()
+        q_copies[h, 3] = remote(qs.at[h, 2], qs.at[h, 3], q_s.at[h, 2], q_r.at[h, 2], at_z(others[1]))
+        q_copies[h, 3].start()
 
     for copy in local:
         copy.wait()
@@ -95,15 +108,16 @@
         cols = slice(h * HD, (h + 1) * HD)
         keys, values = [], []
         for k in range(RING):
-            if k:
-                kv_copies[h, k].wait_recv()
+            if k == 2:
+                kv_copies[h, "k"].wait_recv()
+                kv_copies[h, "v"].wait_recv()
             fresh = stale_v[k, :, :, cols] + kv[h, k].astype(F32)
             keys.append(fresh[0].astype(BF16))
             values.append(fresh[1].T.astype(BF16))
         keys = jnp.concatenate(keys, axis=0)
         values = jnp.concatenate(values, axis=1)
-        for k in (1, 2, 3, 0):
-            if k:
+        for k in (2, 1, 3, 0):
+            if k in (1, 3):
                 q_copies[h, k].wait_recv()
             scores = lax.dot_general(keys, qs[h, k], (((1,), (1,)), ((), ())), preferred_element_type=F32)
             peak = jnp.max(scores, axis=0, keepdims=True)
@@ -119,7 +133,7 @@
             buffer[h, k, HD:, :] = stats.astype(BF16)
             if k:
                 o_copies[h, k] = remote(
-                    part_out.at[h, k], part_in.at[h, k], o_s.at[h, k - 1], o_r.at[h, k - 1], at_z(RING - k)
+                    part_out.at[h, k], part_in.at[h, k], o_s.at[h, k - 1], o_r.at[h, k - 1], at_z(others[k])
                 )
                 o_copies[h, k].start()
 
@@ -164,37 +178,57 @@
         sib_copies[j].wait_recv()
         pair = own[:, :, cols] + sib_in[j].astype(F32).reshape(RING, 16, WIDTH)
         own[:, :, cols] = pair
-        y_out[j] = pair.astype(BF16)
-        for k in (1, 2, 3):
-            y_copies[j, k] = remote(
-                y_out.at[j, lax.rem(y + k, RING)], y_in.at[j, k - 1], y_s.at[j, k - 1], y_r.at[j, k - 1], at_y(k)
-            )
-            y_copies[j, k].start()
+        for i in range(2):
+            y_out[j, i] = pair[:, :, i * HALF : (i + 1) * HALF].astype(BF16)
+        opposite = lax.rem(y + 2, RING)
+        for i, step in enumerate((1, -1)):
+            y_copies[j, i] = remote(
+                y_out.at[j, i, opposite], y_in.at[j, i], y_s.at[j, i], y_r.at[j, i], at_y(step)
+            )
+            y_copies[j, i].start()
+
+    def direct_y(j):
+        for i, step in enumerate((1, -1)):
+            y_copies[j, 2 + i] = remote(
+                y_out.at[j, 1 - i, lax.rem(y + step + RING, RING)],
+                y_in.at[j, 2 + i], y_s.at[j, 2 + i], y_r.at[j, 2 + i], at_y(step),
+            )
+            y_copies[j, 2 + i].start()
+
+    def relay_y(j):
+        for i, step in enumerate((1, -1)):
+            place = lax.rem(y + step + RING, RING)
+            y_copies[j, i].wait_recv()
+            start = j * WIDTH + i * HALF
+            total = own[place, :, start : start + HALF] + y_in[j, i].astype(F32)
+            y_sum[j, i] = total.astype(BF16)
+            y_copies[j, 4 + i] = remote(
+                y_sum.at[j, i], y_in.at[j, 4 + i], y_s.at[j, 4 + i], y_r.at[j, 4 + i], at_y(step)
+            )
+            y_copies[j, 4 + i].start()
 
     def to_z(j):
-        cols = slice(j * WIDTH, (j + 1) * WIDTH)
-        total = own[y, :, cols]
-        for k in (1, 2, 3):
-            y_copies[j, k].wait_recv()
-            total = total + y_in[j, k - 1].astype(F32)
-        z_own[0, :, cols] = total[:8]
-        z_own[1, :, cols] = total[8:]
-        half = WIDTH // 2
-        away = z_own[1 - z_hi, :, cols]
-        z_out[j] = jnp.concatenate([away[:, :half], away[:, half:]], axis=0).astype(BF16)
+        for i in range(2):
+            y_copies[j, 4 + i].wait_recv()
+            y_copies[j, 3 - i].wait_recv()
+            start = j * WIDTH + i * HALF
+            total = own[y, :, start : start + HALF] + y_in[j, 4 + i].astype(F32) + y_in[j, 3 - i].astype(F32)
+            z_own[0, :, start : start + HALF] = total[:8]
+            z_own[1, :, start : start + HALF] = total[8:]
+        away = z_own[1 - z_hi, :, j * WIDTH : (j + 1) * WIDTH]
+        z_out[j] = jnp.concatenate([away[:, :HALF], away[:, HALF:]], axis=0).astype(BF16)
         z_copies[j] = remote(z_out.at[j], z_in.at[j], z_s.at[j], z_r.at[j], across)
         z_copies[j].start()
 
     def finish(j):
         z_copies[j].wait_recv()
-        half = WIDTH // 2
         for i in range(2):
-            cols = slice(j * WIDTH + i * half, j * WIDTH + (i + 1) * half)
+            cols = slice(j * WIDTH + i * HALF, j * WIDTH + (i + 1) * HALF)
             came = z_in[j].astype(F32)[i * 8 : (i + 1) * 8]
             out_ref[:, cols] = (z_own[z_hi, :, cols] + came).astype(BF16)
 
-    stages = (project, to_y, to_z, finish)
-    lags = (0, 2, 6, 8)
+    stages = (project, to_y, direct_y, relay_y, to_z, finish)
+    lags = (0, 1, 3, 4, 7, 11)
     for t in range(CHUNKS + lags[-1]):
         for stage, lag in zip(stages, lags):
             if 0 <= t - lag < CHUNKS:
@@ -210,7 +244,7 @@
     return pl.pallas_call(
         kernel,
         name="sublayer",
-        out_shape=jax.ShapeDtypeStruct((8, D), BF16),
+        out_shape=pltpu.VMEM((8, D), BF16),
         in_specs=[pl.BlockSpec(memory_space=pl.ANY)] * 4,
         out_specs=pl.BlockSpec(memory_space=pltpu.VMEM),
         scratch_shapes=[
@@ -224,29 +258,30 @@
             pltpu.VMEM((RING, 16, D), F32),
             pltpu.VMEM((CHUNKS, 64, WIDTH), BF16),
             pltpu.VMEM((CHUNKS, 64, WIDTH), BF16),
-            pltpu.VMEM((CHUNKS, RING, 16, WIDTH), BF16),
-            pltpu.VMEM((CHUNKS, RING - 1, 16, WIDTH), BF16),
+            pltpu.VMEM((CHUNKS, 2, RING, 16, HALF), BF16),
+            pltpu.VMEM((CHUNKS, 6, 16, HALF), BF16),
+            pltpu.VMEM((CHUNKS, 2, 16, HALF), BF16),
             pltpu.VMEM((2, 8, D), F32),
             pltpu.VMEM((CHUNKS, 16, WIDTH // 2), BF16),
             pltpu.VMEM((CHUNKS, 16, WIDTH // 2), BF16),
             dma((11,)),
-            dma((HEADS, 3)),
-            dma((HEADS, 3)),
-            dma((HEADS, 3)),
-            dma((HEADS, 3)),
-            dma((HEADS, 3)),
-            dma((HEADS, 3)),
-            dma((CHUNKS,)),
-            dma((CHUNKS,)),
-            dma((CHUNKS, 3)),
-            dma((CHUNKS, 3)),
+            dma((HEADS, 4)),
+            dma((HEADS, 4)),
+            dma((HEADS, 3)),
+            dma((HEADS, 3)),
+            dma((HEADS, 3)),
+            dma((HEADS, 3)),
+            dma((CHUNKS,)),
+            dma((CHUNKS,)),
+            dma((CHUNKS, 6)),
+            dma((CHUNKS, 6)),
             dma((CHUNKS,)),
             dma((CHUNKS,)),
         ],
         compiler_params=pltpu.CompilerParams(
             collective_id=0, has_side_effects=True, vmem_limit_bytes=60 * 1024 * 1024
         ),
-    )(queries, stale_kv, delta_kv, out_weight)
+    )(*[pltpu.with_memory_space_constraint(a, pltpu.HBM) for a in (queries, stale_kv, delta_kv, out_weight)])
 
 
 def solution(mesh):

time: 51 us -> 44.7 us (0.88); the launches traced: 50 us -> 44.4 us
  Pallas kernels: 48.4 us -> 43.7 us
  local copies, waits for them, and re-layouts: 1.54 us -> 0.64 us
    pallas_call x1, Pallas kernels: 48.4 us -> 43.7 us  [body(): pl.pallas_call(kernel, name='sublayer', out_shape=pltpu.VMEM((8, D), BF16...]
    unnamed x1, local copies, waits for them, and re-layouts: 1.54 us -> 0.64 us
where the time goes in v2:
time: 44.7 us; the launch traced here: 44.4 us
  Pallas kernels  43.7 us (98%)
  local copies, waits for them, and re-layouts  0.64 us (1%)
    pallas_call x1, Pallas kernels, body(): pl.pallas_call(kernel, name='sublayer', out_shape=pltpu.VMEM((8, D), BF16...  43.7 us

profile of v2, /device:TPU:1, one launch (start us, length us, event | category | flops | bytes accessed | tf_op | source)
XLA Modules:
  0.0 44.4 jit_solution(14476852805563795330)
XLA Ops:
  0.0 43.7 %sublayer.1 = bf16[8,6144]{1,0:T(8,128)(2,1)S(1)} custom-call(bf16[128,384]{1,0:T(8,128)(2,1)} %q_ref.1, f32[2,2048,384]{2,1,0:T(8,128)} %stale_ref.1, bf16[2,128,384]{2,1,0:T(8,128)(2,1)} %delta_ref.1, bf16[384,6144]{1,0:T(8,128)(2,1)} %w_ref.1), custom_call_target="tpu_custom_call" | custom-call | tf_op jit(solution)/shard_map/sublayer/pallas_call | solution.py:244
  43.8 0.6 %copy.6 = bf16[8,6144]{1,0:T(8,128)(2,1)} copy(bf16[8,6144]{1,0:T(8,128)(2,1)S(1)} %sublayer.1) | data formatting | bytes 196608

commit v3 on v2

v3 whole, which is shorter than its diff:
```python
import functools
import math

import jax
import jax.numpy as jnp
from jax import lax
from jax.experimental import pallas as pl
from jax.experimental.pallas import tpu as pltpu
from jax.sharding import PartitionSpec as P

MESH = pl.DeviceIdType.MESH
F32, BF16 = jnp.float32, jnp.bfloat16

HD = 128
HEADS = 3
TOK = 128
RING = 4
COLS = HEADS * HD
D = 6144
CHUNKS = 4
SIDE = D // 2
WIDTH = SIDE // CHUNKS
HALF = WIDTH // 2
SCALE = 1.0 / math.sqrt(HD)


def kernel(
    q_ref, stale_ref, delta_ref, w_ref, out_ref,
    stale_v, kv, qs, part_out, part_in, stat_out, stat_in, w_v, att, own, y_out, y_in, y_sum, z_own, z_out, z_in,
    local_sem, kv_s, kv_r, q_s, q_r, o_s, o_r, t_s, t_r, w_s, w_r, a_s, a_r, y_s, y_r, z_s, z_r,
):
    patch, head = lax.axis_index("patch"), lax.axis_index("head")
    z, x = patch // RING, lax.rem(patch, RING)
    z_hi, y, core = head // 8, lax.rem(head // 2, RING), lax.rem(head, 2)

    def at_x(k):
        return (z * RING + lax.rem(x + k + RING, RING), head)

    def at_z(place):
        return (place * RING + x, head)

    def at_y(k):
        return (patch, z_hi * 8 + lax.rem(y + k + RING, RING) * 2 + core)

    others = {1: z + 1 - 2 * lax.rem(z, 2), 2: lax.rem(z + 2, RING), 3: 3 - z}
    sibling = (patch, z_hi * 8 + y * 2 + (1 - core))
    across = (patch, (1 - z_hi) * 8 + y * 2 + core)
    opposite = (patch, (1 - z_hi) * 8 + y * 2 + (1 - core))

    def remote(src, dst, send, recv, device):
        return pltpu.make_async_remote_copy(
            src_ref=src, dst_ref=dst, send_sem=send, recv_sem=recv, device_id=device, device_id_type=MESH
        )

    local = []
    for k in range(RING):
        row = (z * RING + lax.rem(x - k + RING, RING)) * TOK
        local.append(pltpu.make_async_copy(stale_ref.at[:, pl.ds(row, TOK), :], stale_v.at[k], local_sem.at[k]))
    for h in range(HEADS):
        cols = pl.ds(h * HD, HD)
        local.append(pltpu.make_async_copy(delta_ref.at[:, :, cols], kv.at[h, 0], local_sem.at[4 + h]))
        local.append(pltpu.make_async_copy(q_ref.at[:, cols], qs.at[h, 0], local_sem.at[7 + h]))
    side = pl.ds(pl.multiple_of(core * SIDE, SIDE), SIDE)
    other_side = pl.ds(pl.multiple_of((1 - core) * SIDE, SIDE), SIDE)
    weight = pltpu.make_async_copy(w_ref.at[:, side], w_v.at[pl.ds(0, COLS)], local_sem.at[10])
    for copy in local:
        copy.start()
    weight.start()

    barrier = pltpu.get_barrier_semaphore()
    partners = [at_x(1), at_x(-1), at_y(1), at_y(-1)] + [at_z(others[k]) for k in (1, 2, 3)] + [sibling, across, opposite]
    for device in partners:
        pl.semaphore_signal(barrier, inc=1, device_id=device, device_id_type=MESH)
    pl.semaphore_wait(barrier, len(partners))

    kv_copies, q_copies = {}, {}
    for h in range(HEADS):
        cols = pl.ds(h * HD, HD)
        mine, query = delta_ref.at[:, :, cols], q_ref.at[:, cols]
        kv_copies[h, 1] = remote(mine, kv.at[h, 1], kv_s.at[h, 0], kv_r.at[h, 0], at_x(1))
        kv_copies[h, 3] = remote(mine, kv.at[h, 3], kv_s.at[h, 1], kv_r.at[h, 1], at_x(-1))
        for k in (2, 1):
            q_copies[h, k] = remote(query, qs.at[h, k], q_s.at[h, k - 1], q_r.at[h, k - 1], at_z(others[k]))
        q_copies[h, 2].start()
        kv_copies[h, 1].start()
        kv_copies[h, 3].start()
        q_copies[h, 1].start()
    for h in range(HEADS):
        kv_copies[h, 1].wait_recv()
        kv_copies[h, "k"] = remote(kv.at[h, 1, 0], kv.at[h, 2, 0], kv_s.at[h, 2], kv_r.at[h, 2], at_x(1))
        kv_copies[h, "k"].start()
        kv_copies[h, 3].wait_recv()
        kv_copies[h, "v"] = remote(kv.at[h, 3, 1], kv.at[h, 2, 1], kv_s.at[h, 3], kv_r.at[h, 3], at_x(-1))
        kv_copies[h, "v"].start()
        q_copies[h, 2].wait_recv()
        q_copies[h, 3] = remote(qs.at[h, 2], qs.at[h, 3], q_s.at[h, 2], q_r.at[h, 2], at_z(others[1]))
        q_copies[h, 3].start()

    w_copy = remote(w_ref.at[:, other_side], w_v.at[pl.ds(COLS, COLS)], w_s, w_r, sibling)
    w_copy.start()
    for copy in local:
        copy.wait()

    stat_out[...] = jnp.zeros_like(stat_out)
    o_copies = {}
    for h in range(HEADS):
        cols = slice(h * HD, (h + 1) * HD)
        kv_copies[h, "k"].wait_recv()
        kv_copies[h, "v"].wait_recv()
        q_copies[h, 1].wait_recv()
        q_copies[h, 3].wait_recv()
        keys, values = [], []
        for k in range(RING):
            fresh = stale_v[k, :, :, cols] + kv[h, k].astype(F32)
            keys.append(fresh[0].astype(BF16))
            values.append(fresh[1].T.astype(BF16))
        keys = jnp.concatenate(keys, axis=0)
        values = jnp.concatenate(values, axis=1)
        for k in (2, 1, 3, 0):
            scores = lax.dot_general(keys, qs[h, k], (((1,), (1,)), ((), ())), preferred_element_type=F32)
            peak = jnp.max(scores, axis=0, keepdims=True)
            expo = jnp.exp((scores - peak) * SCALE)
            denom = jnp.sum(expo, axis=0, keepdims=True)
            mixed = jnp.dot(values, expo.astype(BF16), preferred_element_type=F32) / denom
            buffer = part_out if k else part_in
            buffer[h, k] = mixed.astype(BF16)
            stat_out[k, h : h + 1, :] = peak * SCALE + jnp.log(denom)
        for k in (2, 3, 1):
            o_copies[h, k] = remote(
                part_out.at[h, k], part_in.at[h, k], o_s.at[h, k - 1], o_r.at[h, k - 1], at_z(others[k])
            )
            o_copies[h, k].start()
            if h == HEADS - 1:
                o_copies["t", k] = remote(
                    stat_out.at[k], stat_in.at[k], t_s.at[k - 1], t_r.at[k - 1], at_z(others[k])
                )
                o_copies["t", k].start()

    logs = [stat_out[0]]
    for k in (1, 2, 3):
        o_copies["t", k].wait_recv()
        logs.append(stat_in[k])
    top = functools.reduce(jnp.maximum, logs)
    shares = [jnp.exp(log - top) for log in logs]
    total = functools.reduce(jnp.add, shares)
    shares = [share / total for share in shares]
    a_copies = {}
    for h in range(HEADS):
        terms = []
        for k in range(RING):
            if k:
                o_copies[h, k].wait_recv()
            terms.append(part_in[h, k].astype(F32) * shares[k][h : h + 1])
        merged = functools.reduce(jnp.add, terms).T
        merged = jnp.concatenate(
            [merged[(zz * 8 + yy * 2 + c) * 8 :][:8] for yy in range(RING) for zz in range(2) for c in range(2)], axis=0
        )
        att[:, h * HD : (h + 1) * HD] = merged.astype(BF16)
        a_copies[h] = remote(
            att.at[:, pl.ds(h * HD, HD)], att.at[:, pl.ds(COLS + h * HD, HD)], a_s.at[h], a_r.at[h], sibling
        )
        a_copies[h].start()

    weight.wait()
    w_copy.wait_recv()
    for h in range(HEADS):
        a_copies[h].wait_recv()
    y_copies, z_copies = {}, {}

    def project(j):
        cols = slice(j * WIDTH, (j + 1) * WIDTH)
        pair = jnp.dot(att[...], w_v[:, cols], preferred_element_type=F32).reshape(RING, 32, WIDTH)
        own[:, :, cols] = pair
        for i in range(2):
            y_out[j, i] = pair[:, :, i * HALF : (i + 1) * HALF].astype(BF16)
        far = lax.rem(y + 2, RING)
        for i, step in enumerate((1, -1)):
            y_copies[j, i] = remote(
                y_out.at[j, i, far], y_in.at[j, i], y_s.at[j, i], y_r.at[j, i], at_y(step)
            )
            y_copies[j, i].start()

    def direct_y(j):
        for i, step in enumerate((1, -1)):
            y_copies[j, 2 + i] = remote(
                y_out.at[j, 1 - i, lax.rem(y + step + RING, RING)],
                y_in.at[j, 2 + i], y_s.at[j, 2 + i], y_r.at[j, 2 + i], at_y(step),
            )
            y_copies[j, 2 + i].start()

    def relay_y(j):
        for i, step in enumerate((1, -1)):
            place = lax.rem(y + step + RING, RING)
            y_copies[j, i].wait_recv()
            start = j * WIDTH + i * HALF
            total = own[place, :, start : start + HALF] + y_in[j, i].astype(F32)
            y_sum[j, i] = total.astype(BF16)
            y_copies[j, 4 + i] = remote(
                y_sum.at[j, i], y_in.at[j, 4 + i], y_s.at[j, 4 + i], y_r.at[j, 4 + i], at_y(step)
            )
            y_copies[j, 4 + i].start()

    def to_z(j):
        for i in range(2):
            y_copies[j, 4 + i].wait_recv()
            y_copies[j, 3 - i].wait_recv()
            start = j * WIDTH + i * HALF
            total = own[y, :, start : start + HALF] + y_in[j, 4 + i].astype(F32) + y_in[j, 3 - i].astype(F32)
            z_own[:, :, :, start : start + HALF] = total.reshape(2, 2, 8, HALF)
        for i, (place, owner, device) in enumerate(
            ((z_hi, 1 - core, sibling), (1 - z_hi, core, across), (1 - z_hi, 1 - core, opposite))
        ):
            away = z_own[place, owner, :, j * WIDTH : (j + 1) * WIDTH]
            z_out[j, i] = jnp.concatenate([away[:, :HALF], away[:, HALF:]], axis=0).astype(BF16)
            z_copies[j, i] = remote(z_out.at[j, i], z_in.at[j, i], z_s.at[j, i], z_r.at[j, i], device)
            z_copies[j, i].start()

    def finish(j):
        for i in range(3):
            z_copies[j, i].wait_recv()
        here, there = z_in[j, 1].astype(F32), z_in[j, 0].astype(F32) + z_in[j, 2].astype(F32)
        for i in range(2):
            start = j * WIDTH + i * HALF
            rows = slice(i * 8, (i + 1) * 8)
            mine = z_own[z_hi, core, :, start : start + HALF] + here[rows]
            out_ref[:, pl.ds(pl.multiple_of(core * SIDE + start, HD), HALF)] = mine.astype(BF16)
            out_ref[:, pl.ds(pl.multiple_of((1 - core) * SIDE + start, HD), HALF)] = there[rows].astype(BF16)

    stages = (project, direct_y, relay_y, to_z, finish)
    lags = (0, 3, 4, 7, 11)
    for t in range(CHUNKS + lags[-1]):
        for stage, lag in zip(stages, lags):
            if 0 <= t - lag < CHUNKS:
                stage(t - lag)

    for copies in (kv_copies, q_copies, o_copies, a_copies, y_copies, z_copies):
        for copy in copies.values():
            copy.wait_send()
    w_copy.wait_send()


def body(queries, stale_kv, delta_kv, out_weight):
    dma = pltpu.SemaphoreType.DMA
    return pl.pallas_call(
        kernel,
        name="sublayer",
        out_shape=pltpu.VMEM((8, D), BF16),
        in_specs=[pl.BlockSpec(memory_space=pl.ANY)] * 4,
        out_specs=pl.BlockSpec(memory_space=pltpu.VMEM),
        scratch_shapes=[
            pltpu.VMEM((RING, 2, TOK, COLS), F32),
            pltpu.VMEM((HEADS, RING, 2, TOK, HD), BF16),
            pltpu.VMEM((HEADS, RING, TOK, HD), BF16),
            pltpu.VMEM((HEADS, RING, HD, TOK), BF16),
            pltpu.VMEM((HEADS, RING, HD, TOK), BF16),
            pltpu.VMEM((RING, 8, TOK), F32),
            pltpu.VMEM((RING, 8, TOK), F32),
            pltpu.VMEM((2 * COLS, SIDE), BF16),
            pltpu.VMEM((TOK, 2 * COLS), BF16),
            pltpu.VMEM((RING, 32, SIDE), F32),
            pltpu.VMEM((CHUNKS, 2, RING, 32, HALF), BF16),
            pltpu.VMEM((CHUNKS, 6, 32, HALF), BF16),
            pltpu.VMEM((CHUNKS, 2, 32, HALF), BF16),
            pltpu.VMEM((2, 2, 8, SIDE), F32),
            pltpu.VMEM((CHUNKS, 3, 16, HALF), BF16),
            pltpu.VMEM((CHUNKS, 3, 16, HALF), BF16),
            dma((11,)),
            dma((HEADS, 4)),
            dma((HEADS, 4)),
            dma((HEADS, 3)),
            dma((HEADS, 3)),
            dma((HEADS, 3)),
            dma((HEADS, 3)),
            dma((3,)),
            dma((3,)),
            dma,
            dma,
            dma((HEADS,)),
            dma((HEADS,)),
            dma((CHUNKS, 6)),
            dma((CHUNKS, 6)),
            dma((CHUNKS, 3)),
            dma((CHUNKS, 3)),
        ],
        compiler_params=pltpu.CompilerParams(
            collective_id=0, has_side_effects=True, vmem_limit_bytes=60 * 1024 * 1024
        ),
    )(*[pltpu.with_memory_space_constraint(a, pltpu.HBM) for a in (queries, stale_kv, delta_kv, out_weight)])


def solution(mesh):
    return jax.shard_map(
        body,
        mesh=mesh,
        in_specs=(
            P("patch", "head"),
            P(None, None, "head"),
            P(None, "patch", "head"),
            P("head", None),
        ),
        out_specs=P(("patch", "head"), None),
        check_vma=False,
    )
```

time: 44.7 us -> 44.5 us (level)
  no operation moved by 1% of the time
where the time goes in v3:
time: 44.5 us; the launch traced here: 44.4 us
  Pallas kernels  43.8 us (98%)
  local copies, waits for them, and re-layouts  0.64 us (1%)
    pallas_call x1, Pallas kernels, body(): pl.pallas_call(kernel, name='sublayer', out_shape=pltpu.VMEM((8, D), BF16...  43.8 us

profile of v3, /device:TPU:1, one launch (start us, length us, event | category | flops | bytes accessed | tf_op | source)
XLA Modules:
  0.0 44.4 jit_solution(1254836904579343257)
XLA Ops:
  0.0 43.8 %sublayer.1 = bf16[8,6144]{1,0:T(8,128)(2,1)S(1)} custom-call(bf16[128,384]{1,0:T(8,128)(2,1)} %q_ref.1, f32[2,2048,384]{2,1,0:T(8,128)} %stale_ref.1, bf16[2,128,384]{2,1,0:T(8,128)(2,1)} %delta_ref.1, bf16[384,6144]{1,0:T(8,128)(2,1)} %w_ref.1), custom_call_target="tpu_custom_call" | custom-call | tf_op jit(solution)/shard_map/sublayer/pallas_call | solution.py:244
  43.8 0.6 %copy.6 = bf16[8,6144]{1,0:T(8,128)(2,1)} copy(bf16[8,6144]{1,0:T(8,128)(2,1)S(1)} %sublayer.1) | data formatting | bytes 196608

commit v4 on v3

--- a/solution.py
+++ b/solution.py
@@ -116,7 +116,7 @@
             values.append(fresh[1].T.astype(BF16))
         keys = jnp.concatenate(keys, axis=0)
         values = jnp.concatenate(values, axis=1)
-        for k in (2, 1, 3, 0):
+        def block(k):
             scores = lax.dot_general(keys, qs[h, k], (((1,), (1,)), ((), ())), preferred_element_type=F32)
             peak = jnp.max(scores, axis=0, keepdims=True)
             expo = jnp.exp((scores - peak) * SCALE)
@@ -125,6 +125,9 @@
             buffer = part_out if k else part_in
             buffer[h, k] = mixed.astype(BF16)
             stat_out[k, h : h + 1, :] = peak * SCALE + jnp.log(denom)
+
+        for k in (2, 1, 3):
+            block(k)
         for k in (2, 3, 1):
             o_copies[h, k] = remote(
                 part_out.at[h, k], part_in.at[h, k], o_s.at[h, k - 1], o_r.at[h, k - 1], at_z(others[k])
@@ -135,6 +138,7 @@
                     stat_out.at[k], stat_in.at[k], t_s.at[k - 1], t_r.at[k - 1], at_z(others[k])
                 )
                 o_copies["t", k].start()
+        block(0)
 
     logs = [stat_out[0]]
     for k in (1, 2, 3):

time: 44.5 us -> 44.6 us (level)
  no operation moved by 1% of the time
where the time goes in v4:
time: 44.6 us
  Pallas kernels  43.9 us (98%)
  local copies, waits for them, and re-layouts  0.64 us (1%)
    pallas_call x1, Pallas kernels, body(): pl.pallas_call(kernel, name='sublayer', out_shape=pltpu.VMEM((8, D), BF16...  43.9 us

profile of v4, /device:TPU:1, one launch (start us, length us, event | category | flops | bytes accessed | tf_op | source)
XLA Modules:
  0.0 44.6 jit_solution(3885514389619313824)
XLA Ops:
  0.0 43.9 %sublayer.1 = bf16[8,6144]{1,0:T(8,128)(2,1)S(1)} custom-call(bf16[128,384]{1,0:T(8,128)(2,1)} %q_ref.1, f32[2,2048,384]{2,1,0:T(8,128)} %stale_ref.1, bf16[2,128,384]{2,1,0:T(8,128)(2,1)} %delta_ref.1, bf16[384,6144]{1,0:T(8,128)(2,1)} %w_ref.1), custom_call_target="tpu_custom_call" | custom-call | tf_op jit(solution)/shard_map/sublayer/pallas_call | solution.py:248
  43.9 0.6 %copy.6 = bf16[8,6144]{1,0:T(8,128)(2,1)} copy(bf16[8,6144]{1,0:T(8,128)(2,1)S(1)} %sublayer.1) | data formatting | bytes 196608

commit v5 on v3

--- a/solution.py
+++ b/solution.py
@@ -63,9 +63,6 @@
     side = pl.ds(pl.multiple_of(core * SIDE, SIDE), SIDE)
     other_side = pl.ds(pl.multiple_of((1 - core) * SIDE, SIDE), SIDE)
     weight = pltpu.make_async_copy(w_ref.at[:, side], w_v.at[pl.ds(0, COLS)], local_sem.at[10])
-    for copy in local:
-        copy.start()
-    weight.start()
 
     barrier = pltpu.get_barrier_semaphore()
     partners = [at_x(1), at_x(-1), at_y(1), at_y(-1)] + [at_z(others[k]) for k in (1, 2, 3)] + [sibling, across, opposite]
@@ -74,7 +71,7 @@
     pl.semaphore_wait(barrier, len(partners))
 
     kv_copies, q_copies = {}, {}
-    for h in range(HEADS):
+    def send_own(h):
         cols = pl.ds(h * HD, HD)
         mine, query = delta_ref.at[:, :, cols], q_ref.at[:, cols]
         kv_copies[h, 1] = remote(mine, kv.at[h, 1], kv_s.at[h, 0], kv_r.at[h, 0], at_x(1))
@@ -85,7 +82,7 @@
         kv_copies[h, 1].start()
         kv_copies[h, 3].start()
         q_copies[h, 1].start()
-    for h in range(HEADS):
+    def send_relays(h):
         kv_copies[h, 1].wait_recv()
         kv_copies[h, "k"] = remote(kv.at[h, 1, 0], kv.at[h, 2, 0], kv_s.at[h, 2], kv_r.at[h, 2], at_x(1))
         kv_copies[h, "k"].start()
@@ -96,8 +93,17 @@
         q_copies[h, 3] = remote(qs.at[h, 2], qs.at[h, 3], q_s.at[h, 2], q_r.at[h, 2], at_z(others[1]))
         q_copies[h, 3].start()
 
+    send_own(0)
+    send_own(1)
+    for copy in local:
+        copy.start()
+    send_relays(0)
+    send_own(2)
+    send_relays(1)
+    send_relays(2)
     w_copy = remote(w_ref.at[:, other_side], w_v.at[pl.ds(COLS, COLS)], w_s, w_r, sibling)
     w_copy.start()
+    weight.start()
     for copy in local:
         copy.wait()
 
@@ -227,7 +233,7 @@
             out_ref[:, pl.ds(pl.multiple_of((1 - core) * SIDE + start, HD), HALF)] = there[rows].astype(BF16)
 
     stages = (project, direct_y, relay_y, to_z, finish)
-    lags = (0, 3, 4, 7, 11)
+    lags = (0, 3, 4, 8, 12)
     for t in range(CHUNKS + lags[-1]):
         for stage, lag in zip(stages, lags):
             if 0 <= t - lag < CHUNKS:

time: 44.5 us -> 44.4 us (level)
  no operation moved by 1% of the time
where the time goes in v5:
time: 44.4 us; the launch traced here: 44.3 us
  Pallas kernels  43.6 us (98%)
  local copies, waits for them, and re-layouts  0.64 us (1%)
    pallas_call x1, Pallas kernels, body(): pl.pallas_call(kernel, name='sublayer', out_shape=pltpu.VMEM((8, D), BF16...  43.6 us

profile of v5, /device:TPU:1, one launch (start us, length us, event | category | flops | bytes accessed | tf_op | source)
XLA Modules:
  0.0 44.3 jit_solution(1993822681059820886)
XLA Ops:
  0.0 43.6 %sublayer.1 = bf16[8,6144]{1,0:T(8,128)(2,1)S(1)} custom-call(bf16[128,384]{1,0:T(8,128)(2,1)} %q_ref.1, f32[2,2048,384]{2,1,0:T(8,128)} %stale_ref.1, bf16[2,128,384]{2,1,0:T(8,128)(2,1)} %delta_ref.1, bf16[384,6144]{1,0:T(8,128)(2,1)} %w_ref.1), custom_call_target="tpu_custom_call" | custom-call | tf_op jit(solution)/shard_map/sublayer/pallas_call | solution.py:250
  43.7 0.6 %copy.6 = bf16[8,6144]{1,0:T(8,128)(2,1)} copy(bf16[8,6144]{1,0:T(8,128)(2,1)S(1)} %sublayer.1) | data formatting | bytes 196608
